TPU v7x, 128 devices: a whole 4x4x4 slice. The times are simulated.
128 devices in a mesh: queue: 16 (over z, y_hi, core), tensor: 8 (over x, y_lo).
Axes of the slice: x: 4, y: 4 (y_hi: 2, y_lo: 2; y = y_hi * 2 + y_lo), z: 4, core: 2. Of those that a mesh axis runs over, the one named last changes fastest.
Arguments:
- latents: bfloat16 [16, 768, 3072], P('queue'), may hold values from -6 to 6
- levels: int32 [16], P('queue'), may hold values from 0 to 49
- mod_table: bfloat16 [50, 9216], replicated, may hold values from -3 to 3
- step_size: float32 [50], replicated, may hold values from 0.2 to 1
- qkv_weight: bfloat16 [3, 3072, 3072], P(None, None, 'tensor'), may hold values from -0.109375 to 0.109375
- q_gain: float32 [128], replicated, may hold values from 0.8 to 4, as said below
- k_gain: float32 [128], replicated, may hold values from 0.8 to 4, as said below
- out_weight: bfloat16 [3072, 3072], P('tensor'), may hold values from -0.109375 to 0.109375
- fresh_noise: bfloat16 [2, 768, 3072], P(None, 'tensor'), may hold values from -6 to 6
Outputs:
- queue_out: bfloat16 [16, 768, 3072], P('queue')
Inputs may be any that keep to these rules, and one draw needn't show every extreme that they name: `q_gain`: positive gains. `k_gain`: positive gains.
All inputs are finite; a program needn't handle non-finite values.
Results may differ from a plain program's by a relative error of at most 0.03.
Values may be sent and summed in bfloat16 or wider, within the bound.
A program may use at most 128 MiB of HBM per device.

v0:
```python
import jax
import jax.numpy as jnp
from jax import lax
from jax.sharding import PartitionSpec as P

HD = 128
STEPS = 2


def shifted(block, axis, distance):
    devices = range(lax.axis_size(axis))
    route = [(i - distance, i) for i in devices if i - distance in devices]
    return lax.ppermute(block, axis, route)


def normalize(values, epsilon):
    return values * lax.rsqrt(jnp.mean(values * values, axis=-1, keepdims=True) + epsilon)


def body(
    latents, levels, mod_table, step_size, qkv_weight, q_gain, k_gain, out_weight, fresh_noise
):
    frame_rows = latents.shape[1]
    model_width = latents.shape[2]
    head_cols = qkv_weight.shape[2]
    heads_here = head_cols // HD
    first_owner = lax.axis_index("queue") == 0
    onehot = (jnp.arange(mod_table.shape[0], dtype=jnp.int32) == levels[0]).astype(jnp.bfloat16)
    modulation = jnp.dot(onehot[None, :], mod_table, preferred_element_type=jnp.float32)[0]
    rate = jnp.sum(onehot.astype(jnp.float32) * step_size)
    shift_vec = modulation[:model_width]
    scale_vec = modulation[model_width : 2 * model_width]
    gate_vec = modulation[2 * model_width :]
    key_valid = jnp.logical_or(
        jnp.arange(2 * frame_rows) >= frame_rows, jnp.logical_not(first_owner)
    )
    noise_full = lax.all_gather(fresh_noise, "tensor", axis=1, tiled=True)
    frame = latents[0]
    for step_index in range(STEPS):
        arrived = shifted(frame, "queue", 1)
        frame = jnp.where(first_owner, noise_full[step_index], arrived)
        state = frame.astype(jnp.float32)
        normed = (normalize(state, 1e-06) * (1.0 + scale_vec) + shift_vec).astype(jnp.bfloat16)
        query = jnp.dot(normed, qkv_weight[0], preferred_element_type=jnp.float32).reshape(
            frame_rows, heads_here, HD
        )
        keys = jnp.dot(normed, qkv_weight[1], preferred_element_type=jnp.float32).reshape(
            frame_rows, heads_here, HD
        )
        values = jnp.dot(normed, qkv_weight[2], preferred_element_type=jnp.float32).astype(
            jnp.bfloat16
        )
        query = (normalize(query, 1e-06) * q_gain).astype(jnp.bfloat16)
        keys = (normalize(keys, 1e-06) * k_gain).astype(jnp.bfloat16)
        key_value = jnp.stack([keys.reshape(frame_rows, head_cols), values], axis=0)
        earlier = shifted(key_value, "queue", 1)
        all_keys = jnp.concatenate([earlier[0], key_value[0]], axis=0).reshape(
            2 * frame_rows, heads_here, HD
        )
        all_values = jnp.concatenate([earlier[1], key_value[1]], axis=0).reshape(
            2 * frame_rows, heads_here, HD
        )
        scores = jnp.einsum("qhd,khd->hqk", query, all_keys, preferred_element_type=jnp.float32)
        scores = scores * (1.0 / jnp.sqrt(jnp.float32(HD)))
        scores = jnp.where(key_valid[None, None, :], scores, jnp.float32(-1e30))
        row_top = jnp.max(scores, axis=-1, keepdims=True)
        raised = jnp.exp(scores - row_top)
        weights = (raised / jnp.sum(raised, axis=-1, keepdims=True)).astype(jnp.bfloat16)
        attended = jnp.einsum(
            "hqk,khd->qhd", weights, all_values, preferred_element_type=jnp.float32
        )
        attended = attended.astype(jnp.bfloat16).reshape(frame_rows, head_cols)
        partial_term = jnp.dot(attended, out_weight, preferred_element_type=jnp.float32)
        update = lax.psum(partial_term.astype(jnp.bfloat16), "tensor").astype(jnp.float32)
        frame = (state + rate * gate_vec * update).astype(jnp.bfloat16)
    return frame[None]


def solution(mesh):
    return jax.shard_map(
        body,
        mesh=mesh,
        in_specs=(
            P("queue", None, None),
            P("queue"),
            P(),
            P(),
            P(None, None, "tensor"),
            P(),
            P(),
            P("tensor", None),
            P(None, "tensor", None),
        ),
        out_specs=P("queue", None, None),
        check_vma=False,
    )
```

profile of v0, /device:TPU:16, one launch (start us, length us, event | category | flops | bytes accessed | tf_op | source)
XLA Modules:
  0.0 843.3 jit_solution(9945534163494660090)
XLA Ops:
  6.5 0.0 copy-start
  6.5 0.0 all-gather.2.cloned.1.call-start
  6.5 0.7 all-gather.2.cloned.1.call-update
  7.3 0.0 all-reduce.3.cloned.1.call-start
  7.3 1.9 collective-permute-start
  9.9 5.0 slice_bitcast_fusion.2
  14.9 4.4 copy.10
  19.3 0.0 copy-done.14
  19.3 0.6 fusion.66
  19.9 0.0 copy-done.6
  19.9 0.3 fusion.60
  20.2 0.7 slice_multiply_fusion
  20.9 0.0 copy-start.7
  20.9 0.0 copy-start.9
  20.9 219.8 %collective-permute-done = bf16[768,3072]{1,0:T(8,128)(2,1)} collective-permute-done((bf16[768,3072]{1,0:T(8,128)(2,1)}, bf16[768,3072]{1,0:T(8,128)(2,1)}, u32[]{:S(2)}, u32[]{:S(2)}) %collective-permute-start) | collective-permute-done | bytes 4718624 | tf_op jit(solution)/shard_map/ppermute | solution.py:13
  240.7 1.6 all-gather.2.cloned.1.call-done
  242.4 6.0 fusion.4
  248.4 0.0 copy-start.1
  248.4 0.0 copy-start.3
  248.4 5.9 fusion.43
  254.3 0.0 copy-done.7
  254.4 0.0 copy-start.12
  254.4 2.3 multiply_reduce_fusion.3
  256.7 0.1 multiply_convert_fusion.3
  256.9 1.2 pad_maximum_fusion
  258.0 2.1 collective-permute-start.1
  260.2 4.3 copy.11
  264.4 0.6 fusion.59
  265.0 6.3 multiply_reduce_fusion.2
  271.3 0.6 add_rsqrt_fusion.2
  272.0 5.4 collective-permute-done.1
  277.4 2.4 fusion.91
  279.8 11.6 %fusion.92 = (f32[3,768]{1,0:T(4,128)}, f32[3,768,1536]{2,1,0:T(8,128)}) fusion(pred[1536]{0:T(1024)(128)(4,1)} %fusion.59, bf16[768,3,128]{0,2,1:T(8,128)(2,1)S(1)} %multiply_convert_fusion.3, bf16[768,3,128]{0,2,1:T(8,128)(2,1)} %bitcast.95, f32[768,3,128]{0,2,1:T(8,128)} %get-tuple-element.21, f32[128]{0:T(128)} %param.14, f32[768,3]{0,1:T(4,128)} %add_rsqrt_fusion.2), kind=kOutput, calls=%fused_computation.114 | convolution fusion | flops 923371008 | bytes 16535552 | tf_op jit(solution)/shard_map/sub | solution.py:67
  291.4 7.6 fusion.50
  299.0 0.0 copy-done
  299.0 4.4 convolution_convert_fusion.1
  303.5 0.0 all-reduce.3.cloned.1.call-update
  303.5 0.3 all-reduce.5.cloned.1.call-start
  303.7 202.9 %all-reduce.3.cloned.1.call-done = bf16[768,3072]{1,0:T(8,128)(2,1)} async-done(((bf16[768,3072]{1,0:T(8,128)(2,1)}), bf16[768,3072]{1,0:T(8,128)(2,1)}) %all-reduce.3.cloned.1.call-update) | async-done | bytes 4718608 | tf_op jit(solution)/shard_map/psum | solution.py:74
  506.6 5.8 fusion.8
  512.5 2.1 collective-permute-start.2
  514.5 55.0 %collective-permute-done.2 = bf16[768,3072]{1,0:T(8,128)(2,1)S(1)} collective-permute-done((bf16[768,3072]{1,0:T(8,128)(2,1)S(1)}, bf16[768,3072]{1,0:T(8,128)(2,1)S(1)}, u32[]{:S(2)}, u32[]{:S(2)}) %collective-permute-start.2) | collective-permute-done | bytes 4718624 | tf_op jit(solution)/shard_map/ppermute | solution.py:13
  569.6 4.6 fusion.9
  574.2 0.0 copy-done.4
  574.2 0.0 copy-done.8
  574.2 0.0 copy-done.10
  574.2 2.3 multiply_reduce_fusion.1
  576.5 0.0 copy-start.13
  576.6 4.3 fusion.46
  580.9 0.0 copy-done.13
  580.9 0.1 multiply_convert_fusion.1
  581.0 0.1 pad_maximum_fusion.2
  581.2 0.0 copy-start.11
  581.2 2.2 collective-permute-start.3
  583.4 3.3 multiply_reduce_fusion
  586.7 0.6 add_rsqrt_fusion
  587.3 12.9 %collective-permute-done.3 = bf16[2,768,384]{1,2,0:T(8,128)(2,1)S(1)} collective-permute-done((bf16[2,768,384]{1,2,0:T(8,128)(2,1)S(1)}, bf16[2,768,384]{1,2,0:T(8,128)(2,1)S(1)}, u32[]{:S(2)}, u32[]{:S(2)}) %collective-permute-start.3) | collective-permute-done | bytes 1179680 | tf_op jit(solution)/shard_map/ppermute | solution.py:13
  600.2 1.1 fusion.90
  601.3 11.6 %fusion.93 = (f32[3,768]{1,0:T(4,128)}, f32[3,768,1536]{2,1,0:T(8,128)}) fusion(pred[1536]{0:T(1024)(128)(4,1)S(1)} %copy-done.11, bf16[768,3,128]{0,2,1:T(8,128)(2,1)S(1)} %multiply_convert_fusion.1, bf16[768,3,128]{0,2,1:T(8,128)(2,1)} %bitcast.94, f32[768,3,128]{0,2,1:T(8,128)} %get-tuple-element.27, f32[768,3]{0,1:T(4,128)} %add_rsqrt_fusion, ...), kind=kOutput, calls=%fused_computation.115 | convolution fusion | flops 923371008 | bytes 16535552 | tf_op jit(solution)/shard_map/sub | solution.py:67
  612.9 7.6 fusion.49
  620.6 4.3 convolution_convert_fusion
  624.8 0.0 all-reduce.5.cloned.1.call-update
  624.9 203.5 %all-reduce.5.cloned.1.call-done = bf16[768,3072]{1,0:T(8,128)(2,1)} async-done(((bf16[768,3072]{1,0:T(8,128)(2,1)}), bf16[768,3072]{1,0:T(8,128)(2,1)}) %all-reduce.5.cloned.1.call-update) | async-done | bytes 4718608 | tf_op jit(solution)/shard_map/psum | solution.py:74
  828.3 8.0 fusion.22
  (18 shorter events, 0.1 us)
Async XLA Ops:
  6.5 292.5 %copy-start = (bf16[384,3072]{1,0:T(8,128)(2,1)S(1)}, bf16[384,3072]{1,0:T(8,128)(2,1)}, u32[]{:S(2)}) copy-start(bf16[384,3072]{1,0:T(8,128)(2,1)} %param.16) | copy-start | bytes 7077892
  6.5 235.8 %all-gather.2.cloned.1.call-start = ((), (), s32[]{:S(2)}) async-start(), calls=%async_computation | async-start | bytes 10616832 | tf_op jit(solution)/shard_map/all_gather | solution.py:37
  7.3 499.4 %all-reduce.3.cloned.1.call-start = ((), (), s32[]{:S(2)}) async-start(), calls=%async_computation.1 | async-start | bytes 9437184 | tf_op jit(solution)/shard_map/psum | solution.py:74
  7.3 233.4 %collective-permute-start = (bf16[768,3072]{1,0:T(8,128)(2,1)}, bf16[768,3072]{1,0:T(8,128)(2,1)}, u32[]{:S(2)}, u32[]{:S(2)}) collective-permute-start(bf16[768,3072]{1,0:T(8,128)(2,1)} %bitcast.97), channel_id=1, source_target_pairs={{0,8},{8,16},{16,24},{24,32},{32,40},{40,48},{48,56},{56,64},{64,7... | collective-permute-start | bytes 14155784 | tf_op jit(solution)/shard_map/ppermute | solution.py:13
  14.9 4.4 copy-start.14
  14.9 5.0 copy-start.6
  20.9 233.4 %copy-start.7 = (f32[3072]{0:T(1024)}, f32[3072]{0:T(1024)S(1)}, u32[]{:S(2)}) copy-start(f32[3072]{0:T(1024)S(1)} %get-tuple-element.16) | copy-start | bytes 36868
  20.9 233.4 %copy-start.9 = (f32[3072]{0:T(1024)}, f32[3072]{0:T(1024)S(1)}, u32[]{:S(2)}) copy-start(f32[3072]{0:T(1024)S(1)} %get-tuple-element.17) | copy-start | bytes 36868
  248.4 6.0 copy-start.1
  248.4 5.9 copy-start.3
  254.4 2.3 copy-start.12
  258.0 19.3 %collective-permute-start.1 = (bf16[2,768,384]{1,2,0:T(8,128)(2,1)}, bf16[2,768,384]{1,2,0:T(8,128)(2,1)}, u32[]{:S(2)}, u32[]{:S(2)}) collective-permute-start(bf16[2,768,384]{1,2,0:T(8,128)(2,1)} %pad_maximum_fusion), channel_id=1, source_target_pairs={{0,8},{8,16},{16,24},{24,32},{32,40},{40,48},{48,56},{56,64},{64,7... | collective-permute-start | bytes 3538952 | tf_op jit(solution)/shard_map/ppermute | solution.py:13
  303.5 524.9 %all-reduce.5.cloned.1.call-start = ((), (), s32[]{:S(2)}) async-start(), calls=%async_computation.2 | async-start | bytes 9437184 | tf_op jit(solution)/shard_map/psum | solution.py:74
  512.4 61.8 %copy-start.4 = (bf16[384,3072]{1,0:T(8,128)(2,1)S(1)}, bf16[384,3072]{1,0:T(8,128)(2,1)}, u32[]{:S(2)}) copy-start(bf16[384,3072]{1,0:T(8,128)(2,1)} %copy.10) | copy-start | bytes 7077892
  512.5 61.8 %copy-start.8 = (f32[3072]{0:T(1024)S(1)}, f32[3072]{0:T(1024)}, u32[]{:S(2)}) copy-start(f32[3072]{0:T(1024)} %copy-done.7) | copy-start | bytes 36868
  512.5 61.8 %copy-start.10 = (f32[3072]{0:T(1024)S(1)}, f32[3072]{0:T(1024)}, u32[]{:S(2)}) copy-start(f32[3072]{0:T(1024)} %copy-done.9) | copy-start | bytes 36868
  512.5 57.1 %collective-permute-start.2 = (bf16[768,3072]{1,0:T(8,128)(2,1)S(1)}, bf16[768,3072]{1,0:T(8,128)(2,1)S(1)}, u32[]{:S(2)}, u32[]{:S(2)}) collective-permute-start(bf16[768,3072]{1,0:T(8,128)(2,1)S(1)} %fusion.8), channel_id=1, source_target_pairs={{0,8},{8,16},{16,24},{24,32},{32,40},{40,48},{48,56},{56,64},{64,7... | collective-permute-start | bytes 14155784 | tf_op jit(solution)/shard_map/ppermute | solution.py:13
  574.2 9.2 %copy-start.2 = (bf16[768,3072]{1,0:T(8,128)(2,1)}, bf16[768,3072]{1,0:T(8,128)(2,1)S(1)}, u32[]{:S(2)}) copy-start(bf16[768,3072]{1,0:T(8,128)(2,1)S(1)} %get-tuple-element.6) | copy-start | bytes 14155780
  576.5 4.4 copy-start.13
  576.5 6.8 copy-start.5
  581.2 20.1 %copy-start.11 = (pred[1536]{0:T(1024)(128)(4,1)S(1)}, pred[1536]{0:T(1024)(128)(4,1)}, u32[]{:S(2)}) copy-start(pred[1536]{0:T(1024)(128)(4,1)} %fusion.59) | copy-start | bytes 4612
  581.2 19.0 %collective-permute-start.3 = (bf16[2,768,384]{1,2,0:T(8,128)(2,1)S(1)}, bf16[2,768,384]{1,2,0:T(8,128)(2,1)S(1)}, u32[]{:S(2)}, u32[]{:S(2)}) collective-permute-start(bf16[2,768,384]{1,2,0:T(8,128)(2,1)S(1)} %pad_maximum_fusion.2), channel_id=1, source_target_pairs={{0,8},{8,16},{16,24},{24,32},{32,40},{40,48},{48,56},{56,64},{64,7... | collective-permute-start | bytes 3538952 | tf_op jit(solution)/shard_map/ppermute | solution.py:13
Sparse Core Ops, SparseCore 0:
  9.0 233.3 all-gather.1
  303.6 202.9 all-reduce.2
  625.0 203.3 all-reduce.4
where the time goes:
time: 852 us; the launch traced here: 843 us
  waiting for transfers between devices  702 us (82%)
  matrix products  71.9 us (8%)
  other arithmetic  29.1 us (3%)
  local copies, waits for them, and re-layouts  17.3 us (2%)
  between operations  14.6 us (2%)
  starting transfers between devices  8.56 us (1%)
    psum x2, waiting for transfers between devices, body(): lax.psum(partial_term.astype(jnp.bfloat16), 'tensor').astype(jnp.float32)  406 us
    ppermute x4, waiting for transfers between devices, shifted(): return lax.ppermute(block, axis, route)  293 us
    sub x2, matrix products, body(): raised = jnp.exp(scores - row_top)  23.2 us
  transfers between devices with their start and end apart: 7, of which 7 were waited for; matrix products, arithmetic and copies ran while one was open for 3% of the time, Pallas kernels for 0%

commit v1 on v0

v1 whole, which is shorter than its diff:
```python
import functools
import math

import jax
import jax.numpy as jnp
from jax import lax
from jax.experimental import pallas as pl
from jax.experimental.pallas import tpu as pltpu
from jax.sharding import PartitionSpec as P

HD = 128
STEPS = 2
CHUNKS = 2
MESH = pl.DeviceIdType.MESH
NOISE_FROM = {1: 15, 2: 15, 3: 3, 4: 11, 5: 2, 6: 15, 7: 13}


def dot(a, b):
    return jnp.dot(a, b, preferred_element_type=jnp.float32)


def kernel(
    lat, noise, wqkv, wout, mod_own, gains, out,
    frame0, frame1, frame2, normed, wkv, wq, wo, q_buf, kv, kv_prev, mod_next,
    acc, top, total, att, att_all, own_part, part_send, part_recv, z_send,
    load_sem, send_sem, recv_sem,
):
    n_queue, n_tensor = lax.axis_size("queue"), lax.axis_size("tensor")
    n_x = n_tensor // 2
    q, t = lax.axis_index("queue"), lax.axis_index("tensor")
    x, y = t // 2, t % 2
    core = q % 2
    chunks, chunk_rows, width = frame0.shape
    rows = chunk_rows // n_tensor
    cols = wq.shape[1]
    heads = cols // HD
    half = width // 2
    last = n_queue - 1
    noise_from = {k: (v if v <= last else last) for k, v in NOISE_FROM.items()}

    def dev(queue=None, tensor=None):
        return {"queue": q if queue is None else queue, "tensor": t if tensor is None else tensor}

    def tensor_of(xx, yy):
        return lax.rem(xx + n_x, n_x) * 2 + yy

    def queue_at(d):
        return lax.rem(q + d + n_queue, n_queue)

    counter = [0]
    sent = []

    def remote(src, dst, to, keep=True):
        i = counter[0]
        counter[0] += 1
        copy = pltpu.make_async_remote_copy(
            src_ref=src, dst_ref=dst, send_sem=send_sem.at[i], recv_sem=recv_sem.at[i],
            device_id=to, device_id_type=MESH,
        )
        if keep:
            sent.append(copy)
        return copy

    def block(owner):
        return pl.ds(pl.multiple_of(owner * rows, 16), rows)

    barrier = pltpu.get_barrier_semaphore()
    partners = [dev(tensor=jnp.bitwise_xor(t, k)) for k in range(1, n_tensor)]
    steps_q = sorted({d % n_queue for d in (1, -1, 2, -2)} - {0})
    partners += [dev(queue=queue_at(d)) for d in steps_q]
    for partner in partners:
        pl.semaphore_signal(barrier, inc=1, device_id=partner, device_id_type=MESH)
    extra = {k: v for k, v in noise_from.items() if v != last}
    for k, v in extra.items():

        @pl.when(q == v)
        def _():
            pl.semaphore_signal(
                barrier, inc=1, device_id=dev(last, jnp.bitwise_xor(t, k)), device_id_type=MESH
            )

        @pl.when(q == last)
        def _():
            pl.semaphore_signal(
                barrier, inc=1, device_id=dev(v, jnp.bitwise_xor(t, k)), device_id_type=MESH
            )

    def load(src, dst, i):
        return pltpu.make_async_copy(src, dst, load_sem.at[i])

    def lat_rows(ref, owner, c):
        return ref.at[0, pl.ds(owner * rows * chunks + c * rows, rows), :]

    own_noise = [
        load(noise.at[0, pl.ds(c * rows, rows), :], frame0.at[c, block(t), :], c)
        for c in range(chunks)
    ]

    @pl.when(q != last)
    def _():
        for owner in range(n_tensor):
            load(lat_rows(lat, owner, 0), frame0.at[0, pl.ds(owner * rows, rows), :], 0).start()

    @pl.when(q == last)
    def _():
        for c in range(chunks):
            own_noise[c].start()

    load_kv = [load(wqkv.at[j + 1], wkv.at[:, pl.ds(j * cols, cols)], chunks + j) for j in range(2)]
    load_q = load(wqkv.at[0], wq, chunks + 2)
    own_wo = pl.ds(pl.multiple_of(x * cols, HD), cols)
    load_o = load(wout, wo.at[own_wo, :], chunks + 3)
    for copy in load_kv:
        copy.start()

    @pl.when(q != last)
    def _():
        for c in range(1, chunks):
            for owner in range(n_tensor):
                load(lat_rows(lat, owner, c), frame0.at[c, pl.ds(owner * rows, rows), :], c).start()

    load_q.start()
    load_o.start()

    arrivals = len(partners)
    for v in extra.values():
        arrivals = arrivals + (q == v).astype(jnp.int32) + (q == last).astype(jnp.int32)
    pl.semaphore_wait(barrier, arrivals)

    send_mod = remote(mod_own, mod_next, dev(queue=queue_at(-1)))
    send_mod.start()
    noise_copies = []
    for c in range(chunks):
        for k in range(1, n_tensor):
            copy = remote(
                noise.at[0, pl.ds(c * rows, rows), :], frame0.at[c, block(t), :],
                dev(last, jnp.bitwise_xor(t, k)), keep=False,
            )
            noise_copies.append((c, k, copy))

            @pl.when(q == noise_from[k])
            def _():
                copy.start()

    core_half = pl.ds(pl.multiple_of(core * half, HD), half)
    quarter = half // 2
    core_quarter = [
        pl.ds(pl.multiple_of(core * half + j * quarter, HD), quarter) for j in range(2)
    ]

    def wo_rows(xx):
        return pl.ds(pl.multiple_of(lax.rem(xx + n_x, n_x) * cols, HD), cols)

    wo_direct = [
        remote(wout.at[:, core_half], wo.at[own_wo, core_half], dev(tensor=tensor_of(x + d, y)))
        for d in (1, -1)
    ]
    for copy in wo_direct:
        copy.start()
    other_core = q + 1 - 2 * core
    wo_far, wo_pass = [], []

    def wo_forward():
        for i, d in enumerate((1, -1)):
            wo_direct[i].wait_recv()
            region = wo.at[wo_rows(x - d), core_quarter[i]]
            copy = remote(region, region, dev(tensor=tensor_of(x + d, y)))
            copy.start()
            wo_far.append(copy)
            region = wo.at[wo_rows(x - d), core_half]
            copy = remote(region, region, dev(queue=other_core))
            copy.start()
            wo_pass.append(copy)

    def wo_finish():
        for i in range(2):
            wo_far[i].wait_recv()
            region = wo.at[wo_rows(x + 2), core_quarter[i]]
            copy = remote(region, region, dev(queue=other_core))
            copy.start()
            wo_pass.append(copy)
        for copy in wo_pass:
            copy.wait_recv()
        load_o.wait()

    def norm_chunk(frame, mod, c):
        tile = rows

        def step(i, _):
            at = pl.ds(pl.multiple_of(i * tile, 16), tile)
            state = frame[c, at, :].astype(jnp.float32)
            scale = lax.rsqrt(jnp.mean(state * state, axis=-1, keepdims=True) + 1e-06)
            normed[c, at, :] = (state * scale * mod[1:2, :] + mod[0:1, :]).astype(jnp.bfloat16)
            return 0

        lax.fori_loop(0, chunk_rows // tile, step, 0)

    def head_norm(part, gain):
        scale = lax.rsqrt(jnp.mean(part * part, axis=-1, keepdims=True) + 1e-06)
        return (part * scale * gain).astype(jnp.bfloat16)

    def project_kv(c):
        at = pl.ds(c * chunk_rows, chunk_rows)
        both = dot(normed[c], wkv[...])
        for h in range(heads):
            lanes = slice(h * HD, (h + 1) * HD)
            kv[0, at, lanes] = head_norm(both[:, lanes], gains[1:2, :])
        kv[1, at, :] = both[:, cols:].astype(jnp.bfloat16)

    def project_q(c):
        part = dot(normed[c], wq[...])
        for h in range(heads):
            lanes = slice(h * HD, (h + 1) * HD)
            q_buf[c, :, lanes] = head_norm(part[:, lanes], gains[0:1, :])

    def send_kv(step, c):
        at = pl.ds(c * chunk_rows, chunk_rows)
        copy = remote(kv.at[:, at, :], kv_prev.at[step, :, at, :], dev(queue=queue_at(1)))
        copy.start()
        return copy

    def scores(c, lanes, keys):
        return lax.dot_general(
            q_buf[c, :, lanes], keys, (((1,), (1,)), ((), ())), preferred_element_type=jnp.float32
        )

    def attend_own(c):
        def one(h, _):
            lanes = pl.ds(pl.multiple_of(h * HD, HD), HD)
            logits = scores(c, lanes, kv[0, :, lanes])
            peak = jnp.max(logits, axis=-1, keepdims=True)
            raised = jnp.exp2(logits - peak)
            top[c, h] = jnp.broadcast_to(peak, (chunk_rows, HD))
            total[c, h] = jnp.broadcast_to(
                jnp.sum(raised, axis=-1, keepdims=True), (chunk_rows, HD)
            )
            acc[c, :, lanes] = dot(raised.astype(jnp.bfloat16), kv[1, :, lanes])
            return 0

        lax.fori_loop(0, heads, one, 0)

    def attend_prev(step, c):
        def one(h, _):
            lanes = pl.ds(pl.multiple_of(h * HD, HD), HD)
            logits = scores(c, lanes, kv_prev[step, 0, :, lanes])
            before = top[c, h]
            peak = jnp.maximum(before[:, 0:1], jnp.max(logits, axis=-1, keepdims=True))
            raised = jnp.exp2(logits - peak)
            fade = jnp.exp2(before - peak)
            weight = total[c, h] * fade + jnp.sum(raised, axis=-1, keepdims=True)
            summed = acc[c, :, lanes] * fade + dot(
                raised.astype(jnp.bfloat16), kv_prev[step, 1, :, lanes]
            )
            att[step, c, :, lanes] = (summed / weight).astype(jnp.bfloat16)
            return 0

        lax.fori_loop(0, heads, one, 0)

    def attend_alone(step, c):
        def one(h, _):
            lanes = pl.ds(pl.multiple_of(h * HD, HD), HD)
            att[step, c, :, lanes] = (acc[c, :, lanes] / total[c, h]).astype(jnp.bfloat16)
            return 0

        lax.fori_loop(0, heads, one, 0)

    def exchange_att(step, c):
        mine = pl.ds(pl.multiple_of(x * cols, HD), cols)
        copies = []
        for d in range(1, n_x):
            xx = lax.rem(x + d, n_x)
            at = pl.ds(pl.multiple_of(xx * 2 * rows, 16), 2 * rows)
            copy = remote(
                att.at[step, c, at, :], att_all.at[step, c, :, mine],
                dev(tensor=tensor_of(xx, y)),
            )
            copy.start()
            copies.append(copy)
        at = pl.ds(pl.multiple_of(x * 2 * rows, 16), 2 * rows)
        att_all[step, c, :, mine] = att[step, c, at, :]
        return copies

    n_tile = 512 if width % 512 == 0 else HD

    def project_out(step, c):
        def one(i, _):
            lanes = pl.ds(pl.multiple_of(i * n_tile, HD), n_tile)
            part = dot(att_all[step, c], wo[:, lanes])
            low, high = part[:rows], part[rows:]
            own_part[c, :, lanes] = jnp.where(y == 0, low, high)
            part_send[step, c, :, lanes] = jnp.where(y == 0, high, low).astype(jnp.bfloat16)
            return 0

        lax.fori_loop(0, width // n_tile, one, 0)
        copy = remote(
            part_send.at[step, c], part_recv.at[step, c], dev(tensor=jnp.bitwise_xor(t, 1))
        )
        copy.start()
        return copy

    def new_state(frame, mod, step, c):
        update = own_part[c] + part_recv[step, c].astype(jnp.float32)
        state = frame[c, block(t), :].astype(jnp.float32)
        return (state + mod[2:3, :] * update).astype(jnp.bfloat16)

    def ring(frame, c, owner, d, lanes):
        region = frame.at[c, block(owner), lanes]
        copy = remote(region, region, dev(tensor=tensor_of(x + d, y)))
        copy.start()
        return copy

    everything = pl.ds(0, width)
    forward_half = {1: pl.ds(0, half), -1: pl.ds(half, half)}
    partner = jnp.bitwise_xor(t, 1)

    def gather_first(frame, c):
        region = frame.at[c, block(t), :]
        across = remote(region, region, dev(tensor=partner))
        across.start()
        return {"across": across, "own": [ring(frame, c, t, d, everything) for d in (1, -1)]}

    def gather_partner(frame, c, state):
        state["across"].wait_recv()
        state["other"] = [ring(frame, c, partner, d, everything) for d in (1, -1)]

    def gather_forward(frame, c, state, which):
        copies = []
        yy = y if which == "own" else 1 - y
        for copy, d in zip(state[which], (1, -1)):
            copy.wait_recv()
            copies.append(ring(frame, c, tensor_of(x - d, yy), d, forward_half[d]))
        state["far_" + which] = copies

    def gather_wait(state):
        for which in ("far_own", "far_other"):
            for copy in state[which]:
                copy.wait_recv()

    def gather_all(frame, states):
        for c in range(chunks):
            gather_partner(frame, c, states[c])
            gather_forward(frame, c, states[c], "own")
        for c in range(chunks):
            gather_forward(frame, c, states[c], "other")

    def attention(step, position_zero, kv_copies):
        for c in range(chunks):
            attend_own(c)
        for copy in kv_copies:
            copy.wait_recv()
        exchanged = []
        for c in range(chunks):

            @pl.when(position_zero)
            def _():
                attend_alone(step, c)

            @pl.when(jnp.logical_not(position_zero))
            def _():
                attend_prev(step, c)

            exchanged.append(exchange_att(step, c))
        return exchanged

    @pl.when(q != last)
    def _():
        pltpu.make_async_copy(frame0.at[0], frame0.at[0], load_sem.at[0]).wait()

    @pl.when(q == last)
    def _():
        for c in range(chunks):
            own_noise[c].wait()
        for c, k, copy in noise_copies:
            copy.wait_recv()

    send_mod.wait_recv()
    norm_chunk(frame0, mod_next, 0)
    for copy in load_kv:
        copy.wait()
    kv_copies = []
    project_kv(0)
    kv_copies.append(send_kv(0, 0))
    for c in range(1, chunks):

        @pl.when(q != last)
        def _():
            pltpu.make_async_copy(frame0.at[c], frame0.at[c], load_sem.at[c]).wait()

        norm_chunk(frame0, mod_next, c)
        project_kv(c)
        kv_copies.append(send_kv(0, c))
    load_q.wait()
    for c in range(chunks):
        project_q(c)
    exchanged = attention(0, q == last, kv_copies)
    wo_forward()
    wo_finish()
    partials = []
    for c in range(chunks):
        for copy in exchanged[c]:
            copy.wait_recv()
        partials.append(project_out(0, c))
    shifted = []
    for c in range(chunks):
        partials[c].wait_recv()
        z_send[c] = new_state(frame0, mod_next, 0, c)
        copy = remote(z_send.at[c], frame1.at[c, block(t), :], dev(queue=queue_at(2)))
        counter[0] -= 1
        entering = remote(
            noise.at[1, pl.ds(c * rows, rows), :], frame1.at[c, block(t), :],
            dev(queue=queue_at(2)), keep=False,
        )

        @pl.when(q == last - 1)
        def _():
            entering.start()

        @pl.when(q != last - 1)
        def _():
            copy.start()

        shifted.append(copy)
    states = []
    for c in range(chunks):
        shifted[c].wait_recv()
        states.append(gather_first(frame1, c))
    gather_all(frame1, states)

    for copy in kv_copies:
        copy.wait_send()
    sent[:] = [copy for copy in sent if all(copy is not done for done in kv_copies)]
    kv_copies = []
    for c in range(chunks):
        gather_wait(states[c])
        norm_chunk(frame1, mod_own, c)
        project_kv(c)
        kv_copies.append(send_kv(1, c))
        project_q(c)
    exchanged = attention(1, q == 0, kv_copies)
    partials = []
    for c in range(chunks):
        for copy in exchanged[c]:
            copy.wait_recv()
        partials.append(project_out(1, c))
    states = []
    for c in range(chunks):
        partials[c].wait_recv()
        frame2[c, block(t), :] = new_state(frame1, mod_own, 1, c)
        states.append(gather_first(frame2, c))
    gather_all(frame2, states)
    stores = []
    for c in range(chunks):
        gather_wait(states[c])
        copy = load(frame2.at[c], out.at[c], c)
        copy.start()
        stores.append(copy)
    for copy in stores:
        copy.wait()
    for copy in sent:
        copy.wait_send()
    for c, k, copy in noise_copies:

        @pl.when(q == noise_from[k])
        def _():
            copy.wait_send()


def body(
    latents, levels, mod_table, step_size, qkv_weight, q_gain, k_gain, out_weight, fresh_noise
):
    frame_rows, width = latents.shape[1:]
    cols = qkv_weight.shape[2]
    heads = cols // HD
    n_tensor = lax.axis_size("tensor")
    chunks = CHUNKS
    chunk_rows = frame_rows // chunks
    rows = chunk_rows // n_tensor
    onehot = (jnp.arange(mod_table.shape[0], dtype=jnp.int32) == levels[0]).astype(jnp.bfloat16)
    modulation = jnp.dot(onehot[None, :], mod_table, preferred_element_type=jnp.float32)
    rate = jnp.sum(onehot.astype(jnp.float32) * step_size)
    shift, scale, gate = jnp.split(modulation, 3, axis=1)
    mod = jnp.concatenate(
        [shift, 1.0 + scale, rate * gate, jnp.zeros((5, width), jnp.float32)], axis=0
    )
    gains = jnp.concatenate(
        [
            (q_gain * (math.log2(math.e) / math.sqrt(HD)))[None],
            k_gain[None],
            jnp.zeros((6, HD), jnp.float32),
        ],
        axis=0,
    )
    bf16, f32 = jnp.bfloat16, jnp.float32
    frame = pltpu.VMEM((chunks, chunk_rows, width), bf16)
    anywhere = pl.BlockSpec(memory_space=pl.ANY)
    vmem = pl.BlockSpec(memory_space=pltpu.VMEM)
    n_copies = 128
    out = pl.pallas_call(
        kernel,
        out_shape=jax.ShapeDtypeStruct((chunks, chunk_rows, width), bf16),
        in_specs=[anywhere, anywhere, anywhere, anywhere, vmem, vmem],
        out_specs=anywhere,
        scratch_shapes=[
            frame, frame, frame, frame,
            pltpu.VMEM((width, 2 * cols), bf16),
            pltpu.VMEM((width, cols), bf16),
            pltpu.VMEM((n_tensor // 2 * cols, width), bf16),
            pltpu.VMEM((chunks, chunk_rows, cols), bf16),
            pltpu.VMEM((2, frame_rows, cols), bf16),
            pltpu.VMEM((STEPS, 2, frame_rows, cols), bf16),
            pltpu.VMEM((8, width), f32),
            pltpu.VMEM((chunks, chunk_rows, cols), f32),
            pltpu.VMEM((chunks, heads, chunk_rows, HD), f32),
            pltpu.VMEM((chunks, heads, chunk_rows, HD), f32),
            pltpu.VMEM((STEPS, chunks, chunk_rows, cols), bf16),
            pltpu.VMEM((STEPS, chunks, 2 * rows, n_tensor // 2 * cols), bf16),
            pltpu.VMEM((chunks, rows, width), f32),
            pltpu.VMEM((STEPS, chunks, rows, width), bf16),
            pltpu.VMEM((STEPS, chunks, rows, width), bf16),
            pltpu.VMEM((chunks, rows, width), bf16),
            pltpu.SemaphoreType.DMA((chunks + 4,)),
            pltpu.SemaphoreType.DMA((n_copies,)),
            pltpu.SemaphoreType.DMA((n_copies,)),
        ],
        compiler_params=pltpu.CompilerParams(
            collective_id=0, has_side_effects=True, vmem_limit_bytes=62 * 1024 * 1024
        ),
        name="denoise",
    )(latents, fresh_noise, qkv_weight, out_weight, mod, gains)
    out = out.reshape(chunks, n_tensor, rows, width).transpose(1, 0, 2, 3)
    return out.reshape(1, frame_rows, width)


def solution(mesh):
    return jax.shard_map(
        body,
        mesh=mesh,
        in_specs=(
            P("queue", None, None),
            P("queue"),
            P(),
            P(),
            P(None, None, "tensor"),
            P(),
            P(),
            P("tensor", None),
            P(None, "tensor", None),
        ),
        out_specs=P("queue", None, None),
        check_vma=False,
    )
```

time: 852 us -> 220 us (0.26)
  waiting for transfers between devices: 702 us -> 0 us
  Pallas kernels: 0 us -> 207 us
  matrix products: 71.9 us -> 0.3 us
  other arithmetic: 29.1 us -> 4.74 us
  between operations: 14.6 us -> 0.76 us
  local copies, waits for them, and re-layouts: 17.3 us -> 5.12 us
  starting transfers between devices: 8.56 us -> 0 us
    psum x2 -> x0, waiting for transfers between devices: 406 us -> none  [body(): lax.psum(partial_term.astype(jnp.bfloat16), 'tensor').astype(jnp.float32)]
    ppermute x4 -> x0, waiting for transfers between devices: 293 us -> none  [shifted(): return lax.ppermute(block, axis, route)]
    pallas_call x0 -> x1, Pallas kernels: none -> 207 us  [body(): pl.pallas_call(kernel, out_shape=jax.ShapeDtypeStruct((chunks, chunk_rows...]
    dot_general x11 -> x1, matrix products: 48.7 us -> 0.3 us  [body(): jnp.dot(onehot[None, :], mod_table, preferred_element_type=jnp.float32)]
    sub x2 -> x0, matrix products: 23.2 us -> none  [body(): raised = jnp.exp(scores - row_top)]
    dot_general x3 -> x0, local copies, waits for them, and re-layouts: 13.7 us -> none  [the longest x2 9.31 us: body(): jnp.dot(normed, qkv_weight[0], preferred_element_type=jnp.float32)]
    reduce_sum x2 -> x0, other arithmetic: 10.6 us -> none  [normalize(): jnp.mean(values * values, axis=-1, keepdims=True) + epsilon]
  transfers between devices with their start and end apart: 7 -> 0, of which waited for: 7 -> 0; matrix products, arithmetic and copies ran while one was open for 3% -> 0% of each run, Pallas kernels for 0% -> 0%
where the time goes in v1:
time: 220 us; the launch traced here: 218 us
  Pallas kernels  207 us (94%)
  local copies, waits for them, and re-layouts  5.12 us (2%)
  other arithmetic  4.74 us (2%)
    pallas_call x1, Pallas kernels, body(): pl.pallas_call(kernel, out_shape=jax.ShapeDtypeStruct((chunks, chunk_rows...  207 us
    transpose x1, local copies, waits for them, and re-layouts, body(): out = out.reshape(chunks, n_tensor, rows, width).transpose(1, 0, 2, 3)  4.96 us

profile of v1, /device:TPU:16, one launch (start us, length us, event | category | flops | bytes accessed | tf_op | source)
XLA Modules:
  0.0 218.0 jit_solution(3049532572448787367)
XLA Ops:
  0.0 0.0 copy-start
  0.7 1.3 fusion.6
  2.1 0.7 multiply_bitcast_fusion
  2.7 0.1 pad.6.clone
  2.8 0.1 pad.2.clone
  2.9 1.3 maximum_maximum_fusion.1.gains
  4.2 0.0 copy-done
  4.2 0.3 fusion
  4.5 0.7 fusion.8
  5.2 0.7 maximum_maximum_fusion.mod_own
  6.0 207.1 %denoise.1 = bf16[2,384,3072]{2,1,0:T(8,128)(2,1)} custom-call(bf16[1,768,3072]{2,1,0:T(8,128)(2,1)} %lat.1, bf16[2,96,3072]{2,1,0:T(8,128)(2,1)} %noise.1, bf16[3,3072,384]{2,1,0:T(8,128)(2,1)} %wqkv.1, bf16[384,3072]{1,0:T(8,128)(2,1)} %wout.1, f32[8,3072]{1,0:T(8,128)} %maximum_maximum_fusion.mod_own, f32[8,128]{1,0:T(8,128)} %maximum_maximum_fusion.1.gains), custom_call_target="tpu_custom_call" | custom-call | tf_op jit(solution)/shard_map/denoise/pallas_call | solution.py:498
  213.1 5.0 %copy.10 = bf16[8,2,48,3072]{3,2,1,0:T(8,128)(2,1)} copy(bf16[8,2,48,3072]{3,2,0,1:T(8,128)(2,1)} %bitcast.15) | data formatting | bytes 9437184 | tf_op jit(solution)/shard_map/transpose | solution.py:530
  (2 shorter events, 0.0 us)
Async XLA Ops:
  0.0 4.2 %copy-start = (bf16[50,9216]{1,0:T(8,128)(2,1)S(1)}, bf16[50,9216]{1,0:T(8,128)(2,1)}, u32[]{:S(2)}) copy-start(bf16[50,9216]{1,0:T(8,128)(2,1)} %param.11) | copy-start | bytes 2764804

commit v2 on v1

--- a/solution.py
+++ b/solution.py
@@ -11,6 +11,9 @@
 HD = 128
 STEPS = 2
 CHUNKS = 2
+PARTS = 2
+LAST_PART = 1536
+LAST_CUT = 1280
 MESH = pl.DeviceIdType.MESH
 NOISE_FROM = {1: 15, 2: 15, 3: 3, 4: 11, 5: 2, 6: 15, 7: 13}
 
@@ -66,10 +69,10 @@
 
     barrier = pltpu.get_barrier_semaphore()
     partners = [dev(tensor=jnp.bitwise_xor(t, k)) for k in range(1, n_tensor)]
-    steps_q = sorted({d % n_queue for d in (1, -1, 2, -2)} - {0})
-    partners += [dev(queue=queue_at(d)) for d in steps_q]
-    for partner in partners:
-        pl.semaphore_signal(barrier, inc=1, device_id=partner, device_id_type=MESH)
+    partners += [dev(queue=queue_at(d)) for d in sorted({1, n_queue - 1})]
+    partners += [dev(queue_at(d), jnp.bitwise_xor(t, 1)) for d in sorted({2, n_queue - 2})]
+    for to in partners:
+        pl.semaphore_signal(barrier, inc=1, device_id=to, device_id_type=MESH)
     extra = {k: v for k, v in noise_from.items() if v != last}
     for k, v in extra.items():
 
@@ -280,68 +283,104 @@
         att_all[step, c, :, mine] = att[step, c, at, :]
         return copies
 
-    n_tile = 512 if width % 512 == 0 else HD
-
-    def project_out(step, c):
+    parts = PARTS
+    part_cols = width // parts
+    n_tile = 512 if part_cols % 512 == 0 else HD
+    units = [(c, k) for c in range(chunks) for k in range(parts)]
+
+    def project_out(step, c, k):
         def one(i, _):
-            lanes = pl.ds(pl.multiple_of(i * n_tile, HD), n_tile)
+            lanes = pl.ds(pl.multiple_of(k * part_cols + i * n_tile, HD), n_tile)
             part = dot(att_all[step, c], wo[:, lanes])
             low, high = part[:rows], part[rows:]
             own_part[c, :, lanes] = jnp.where(y == 0, low, high)
             part_send[step, c, :, lanes] = jnp.where(y == 0, high, low).astype(jnp.bfloat16)
             return 0
 
-        lax.fori_loop(0, width // n_tile, one, 0)
+        lax.fori_loop(0, part_cols // n_tile, one, 0)
+        lanes = pl.ds(k * part_cols, part_cols)
         copy = remote(
-            part_send.at[step, c], part_recv.at[step, c], dev(tensor=jnp.bitwise_xor(t, 1))
+            part_send.at[step, c, :, lanes], part_recv.at[step, c, :, lanes], dev(tensor=partner)
         )
         copy.start()
         return copy
 
-    def new_state(frame, mod, step, c):
-        update = own_part[c] + part_recv[step, c].astype(jnp.float32)
-        state = frame[c, block(t), :].astype(jnp.float32)
-        return (state + mod[2:3, :] * update).astype(jnp.bfloat16)
-
-    def ring(frame, c, owner, d, lanes):
+    def new_state(frame, mod, step, c, k):
+        lanes = pl.ds(k * part_cols, part_cols)
+        update = own_part[c, :, lanes] + part_recv[step, c, :, lanes].astype(jnp.float32)
+        state = frame[c, block(t), lanes].astype(jnp.float32)
+        return (state + mod[2:3, lanes] * update).astype(jnp.bfloat16)
+
+    def move(frame, c, owner, lanes, to):
         region = frame.at[c, block(owner), lanes]
-        copy = remote(region, region, dev(tensor=tensor_of(x + d, y)))
+        copy = remote(region, region, to)
         copy.start()
         return copy
 
-    everything = pl.ds(0, width)
-    forward_half = {1: pl.ds(0, half), -1: pl.ds(half, half)}
     partner = jnp.bitwise_xor(t, 1)
-
-    def gather_first(frame, c):
-        region = frame.at[c, block(t), :]
-        across = remote(region, region, dev(tensor=partner))
-        across.start()
-        return {"across": across, "own": [ring(frame, c, t, d, everything) for d in (1, -1)]}
-
-    def gather_partner(frame, c, state):
-        state["across"].wait_recv()
-        state["other"] = [ring(frame, c, partner, d, everything) for d in (1, -1)]
-
-    def gather_forward(frame, c, state, which):
-        copies = []
-        yy = y if which == "own" else 1 - y
-        for copy, d in zip(state[which], (1, -1)):
-            copy.wait_recv()
-            copies.append(ring(frame, c, tensor_of(x - d, yy), d, forward_half[d]))
-        state["far_" + which] = copies
-
-    def gather_wait(state):
-        for which in ("far_own", "far_other"):
-            for copy in state[which]:
+    WAYS = (1, -1)
+
+    class Gather:
+        def __init__(self, frame, c, k, side, cut):
+            self.frame, self.c, self.side = frame, c, side
+            self.start = k * part_cols
+            self.cut = cut
+
+        def cols(self, low, high):
+            return pl.ds(self.start + low, high - low)
+
+        def ring(self, owner_x, side, d, low, high):
+            owner = tensor_of(owner_x, side)
+            return move(self.frame, self.c, owner, self.cols(low, high), dev(tensor=tensor_of(x + d, y)))
+
+        def cross(self, owner_x, low):
+            owner = tensor_of(owner_x, self.side)
+            return move(self.frame, self.c, owner, self.cols(low, part_cols), dev(tensor=partner))
+
+        def first(self):
+            self.across = self.cross(x, 0)
+            self.own = [self.ring(x, self.side, d, 0, part_cols) for d in WAYS]
+
+        def second(self):
+            self.across.wait_recv()
+            self.other = [self.ring(x, 1 - self.side, d, 0, self.cut) for d in WAYS]
+
+        def forward_own(self):
+            mid = part_cols // 2
+            self.far, self.crossed = [], []
+            for copy, d in zip(self.own, WAYS):
                 copy.wait_recv()
-
-    def gather_all(frame, states):
+                low, high = (0, mid) if d == 1 else (mid, part_cols)
+                self.far.append(self.ring(x - d, self.side, d, low, high))
+                if self.cut < part_cols:
+                    self.crossed.append(self.cross(x - d, self.cut))
+
+        def forward_other(self):
+            mid = self.cut // 2
+            self.far_other = []
+            for copy, d in zip(self.other, WAYS):
+                copy.wait_recv()
+                low, high = (0, mid) if d == 1 else (mid, self.cut)
+                self.far_other.append(self.ring(x - d, 1 - self.side, d, low, high))
+            if self.cut < part_cols:
+                self.far[1].wait_recv()
+                self.crossed.append(self.cross(x + 2, self.cut))
+
+        def wait(self):
+            self.far[0].wait_recv()
+            if self.cut == part_cols:
+                self.far[1].wait_recv()
+            for copy in self.far_other + self.crossed:
+                copy.wait_recv()
+
+    def output_projection(step, exchanged):
+        partials = []
         for c in range(chunks):
-            gather_partner(frame, c, states[c])
-            gather_forward(frame, c, states[c], "own")
-        for c in range(chunks):
-            gather_forward(frame, c, states[c], "other")
+            for copy in exchanged[c]:
+                copy.wait_recv()
+            for k in range(parts):
+                partials.append(project_out(step, c, k))
+        return partials
 
     def attention(step, position_zero, kv_copies):
         for c in range(chunks):
@@ -395,21 +434,18 @@
     exchanged = attention(0, q == last, kv_copies)
     wo_forward()
     wo_finish()
-    partials = []
-    for c in range(chunks):
-        for copy in exchanged[c]:
-            copy.wait_recv()
-        partials.append(project_out(0, c))
-    shifted = []
-    for c in range(chunks):
-        partials[c].wait_recv()
-        z_send[c] = new_state(frame0, mod_next, 0, c)
-        copy = remote(z_send.at[c], frame1.at[c, block(t), :], dev(queue=queue_at(2)))
+    partials = output_projection(0, exchanged)
+
+    def send_shifted(u):
+        c, k = units[u]
+        lanes = pl.ds(k * part_cols, part_cols)
+        partials[u].wait_recv()
+        z_send[c, :, lanes] = new_state(frame0, mod_next, 0, c, k)
+        place = frame1.at[c, block(t), lanes]
+        to = dev(queue_at(2), partner)
+        copy = remote(z_send.at[c, :, lanes], place, to)
         counter[0] -= 1
-        entering = remote(
-            noise.at[1, pl.ds(c * rows, rows), :], frame1.at[c, block(t), :],
-            dev(queue=queue_at(2)), keep=False,
-        )
+        entering = remote(noise.at[1, pl.ds(c * rows, rows), lanes], place, to, keep=False)
 
         @pl.when(q == last - 1)
         def _():
@@ -419,41 +455,69 @@
         def _():
             copy.start()
 
-        shifted.append(copy)
-    states = []
-    for c in range(chunks):
-        shifted[c].wait_recv()
-        states.append(gather_first(frame1, c))
-    gather_all(frame1, states)
+        return copy
+
+    n_units = len(units)
+    shifted = [None] * n_units
+    gathers = [Gather(frame1, c, k, 1 - y, part_cols) for c, k in units]
+
+    def first_after_shift(u):
+        shifted[u].wait_recv()
+        gathers[u].first()
+
+    for tick in range(n_units + 3):
+        if tick < n_units:
+            shifted[tick] = send_shifted(tick)
+        if 0 <= tick - 1 < n_units:
+            first_after_shift(tick - 1)
+        if 0 <= tick - 2 < n_units:
+            gathers[tick - 2].second()
+            gathers[tick - 2].forward_own()
+        if 0 <= tick - 3 < n_units - parts:
+            gathers[tick - 3].forward_other()
 
     for copy in kv_copies:
         copy.wait_send()
     sent[:] = [copy for copy in sent if all(copy is not done for done in kv_copies)]
     kv_copies = []
     for c in range(chunks):
-        gather_wait(states[c])
+        for k in range(parts):
+            gathers[c * parts + k].wait()
         norm_chunk(frame1, mod_own, c)
         project_kv(c)
         kv_copies.append(send_kv(1, c))
+        if c == chunks - 2:
+            for u in range(n_units - parts, n_units):
+                gathers[u].forward_other()
         project_q(c)
     exchanged = attention(1, q == 0, kv_copies)
-    partials = []
-    for c in range(chunks):
-        for copy in exchanged[c]:
-            copy.wait_recv()
-        partials.append(project_out(1, c))
-    states = []
-    for c in range(chunks):
-        partials[c].wait_recv()
-        frame2[c, block(t), :] = new_state(frame1, mod_own, 1, c)
-        states.append(gather_first(frame2, c))
-    gather_all(frame2, states)
+    partials = output_projection(1, exchanged)
+    cut = LAST_CUT if part_cols == LAST_PART else part_cols // 2
+    gathers = [Gather(frame2, c, k, y, cut) for c, k in units]
     stores = []
-    for c in range(chunks):
-        gather_wait(states[c])
+
+    def store(c):
+        for k in range(parts):
+            gathers[c * parts + k].wait()
         copy = load(frame2.at[c], out.at[c], c)
         copy.start()
         stores.append(copy)
+
+    for tick in range(n_units + 2):
+        if tick < n_units:
+            c, k = units[tick]
+            partials[tick].wait_recv()
+            frame2[c, block(t), pl.ds(k * part_cols, part_cols)] = new_state(
+                frame1, mod_own, 1, c, k
+            )
+            gathers[tick].first()
+        if 0 <= tick - 1 < n_units:
+            gathers[tick - 1].second()
+            gathers[tick - 1].forward_own()
+        if 0 <= tick - 2 < n_units:
+            gathers[tick - 2].forward_other()
+    for c in range(chunks):
+        store(c)
     for copy in stores:
         copy.wait()
     for copy in sent:
@@ -494,7 +558,7 @@
     frame = pltpu.VMEM((chunks, chunk_rows, width), bf16)
     anywhere = pl.BlockSpec(memory_space=pl.ANY)
     vmem = pl.BlockSpec(memory_space=pltpu.VMEM)
-    n_copies = 128
+    n_copies = 192
     out = pl.pallas_call(
         kernel,
         out_shape=jax.ShapeDtypeStruct((chunks, chunk_rows, width), bf16),

time: 220 us -> 204 us (0.927)
  Pallas kernels: 207 us -> 193 us
    pallas_call x1, Pallas kernels: 207 us -> 193 us  [body(): pl.pallas_call(kernel, out_shape=jax.ShapeDtypeStruct((chunks, chunk_rows...]
where the time goes in v2:
time: 204 us
  Pallas kernels  193 us (95%)
  local copies, waits for them, and re-layouts  5.12 us (3%)
  other arithmetic  4.74 us (2%)
    pallas_call x1, Pallas kernels, body(): pl.pallas_call(kernel, out_shape=jax.ShapeDtypeStruct((chunks, chunk_rows...  193 us
    transpose x1, local copies, waits for them, and re-layouts, body(): out = out.reshape(chunks, n_tensor, rows, width).transpose(1, 0, 2, 3)  4.96 us

profile of v2, /device:TPU:16, one launch (start us, length us, event | category | flops | bytes accessed | tf_op | source)
XLA Modules:
  0.0 203.6 jit_solution(17421124499973922771)
XLA Ops:
  0.0 0.0 copy-start
  0.7 1.3 fusion.6
  2.1 0.7 multiply_bitcast_fusion
  2.7 0.1 pad.6.clone
  2.8 0.1 pad.2.clone
  2.9 1.3 maximum_maximum_fusion.1.gains
  4.2 0.0 copy-done
  4.2 0.3 fusion
  4.5 0.7 fusion.8
  5.2 0.7 maximum_maximum_fusion.mod_own
  6.0 192.7 %denoise.1 = bf16[2,384,3072]{2,1,0:T(8,128)(2,1)} custom-call(bf16[1,768,3072]{2,1,0:T(8,128)(2,1)} %lat.1, bf16[2,96,3072]{2,1,0:T(8,128)(2,1)} %noise.1, bf16[3,3072,384]{2,1,0:T(8,128)(2,1)} %wqkv.1, bf16[384,3072]{1,0:T(8,128)(2,1)} %wout.1, f32[8,3072]{1,0:T(8,128)} %maximum_maximum_fusion.mod_own, f32[8,128]{1,0:T(8,128)} %maximum_maximum_fusion.1.gains), custom_call_target="tpu_custom_call" | custom-call | tf_op jit(solution)/shard_map/denoise/pallas_call | solution.py:562
  198.7 5.0 %copy.10 = bf16[8,2,48,3072]{3,2,1,0:T(8,128)(2,1)} copy(bf16[8,2,48,3072]{3,2,0,1:T(8,128)(2,1)} %bitcast.15) | data formatting | bytes 9437184 | tf_op jit(solution)/shard_map/transpose | solution.py:594
  (2 shorter events, 0.0 us)
Async XLA Ops:
  0.0 4.2 %copy-start = (bf16[50,9216]{1,0:T(8,128)(2,1)S(1)}, bf16[50,9216]{1,0:T(8,128)(2,1)}, u32[]{:S(2)}) copy-start(bf16[50,9216]{1,0:T(8,128)(2,1)} %param.11) | copy-start | bytes 2764804

commit v3 on v2

--- a/solution.py
+++ b/solution.py
@@ -15,7 +15,7 @@
 LAST_PART = 1536
 LAST_CUT = 1280
 MESH = pl.DeviceIdType.MESH
-NOISE_FROM = {1: 15, 2: 15, 3: 3, 4: 11, 5: 2, 6: 15, 7: 13}
+NOISE_FROM = {1: (15, 15), 2: (15, 15), 3: (3, 3), 4: (11, 11), 5: (2, 10), 6: (15, 15), 7: (13, 13)}
 
 
 def dot(a, b):
@@ -23,8 +23,8 @@
 
 
 def kernel(
-    lat, noise, wqkv, wout, mod_own, gains, out,
-    frame0, frame1, frame2, normed, wkv, wq, wo, q_buf, kv, kv_prev, mod_next,
+    levels, lat, noise, wqkv, wout, mod_table, step_size, q_gain, k_gain, out,
+    frame0, frame1, frame2, normed, wkv, wq, wo, q_buf, kv, kv_prev, mod_own, mod_next, gains,
     acc, top, total, att, att_all, own_part, part_send, part_recv, z_send,
     load_sem, send_sem, recv_sem,
 ):
@@ -39,7 +39,11 @@
     heads = cols // HD
     half = width // 2
     last = n_queue - 1
-    noise_from = {k: (v if v <= last else last) for k, v in NOISE_FROM.items()}
+    noise_from = {
+        (k, c): (v[c % 2] if v[c % 2] <= last else last)
+        for k, v in NOISE_FROM.items()
+        for c in range(chunks)
+    }
 
     def dev(queue=None, tensor=None):
         return {"queue": q if queue is None else queue, "tensor": t if tensor is None else tensor}
@@ -69,12 +73,13 @@
 
     barrier = pltpu.get_barrier_semaphore()
     partners = [dev(tensor=jnp.bitwise_xor(t, k)) for k in range(1, n_tensor)]
-    partners += [dev(queue=queue_at(d)) for d in sorted({1, n_queue - 1})]
+    near = {1, n_queue - 1} | ({4, n_queue - 4} if n_queue > 4 else set())
+    partners += [dev(queue=queue_at(d)) for d in sorted(near)]
     partners += [dev(queue_at(d), jnp.bitwise_xor(t, 1)) for d in sorted({2, n_queue - 2})]
     for to in partners:
         pl.semaphore_signal(barrier, inc=1, device_id=to, device_id_type=MESH)
-    extra = {k: v for k, v in noise_from.items() if v != last}
-    for k, v in extra.items():
+    extra = sorted({(k, v) for (k, _), v in noise_from.items() if v != last})
+    for k, v in extra:
 
         @pl.when(q == v)
         def _():
@@ -125,8 +130,19 @@
     load_q.start()
     load_o.start()
 
+    n_levels = mod_table.shape[0]
+    hot = lax.broadcasted_iota(jnp.int32, (8, n_levels), 1) == levels[0]
+    rate = jnp.sum(jnp.where(hot, step_size[...], 0.0), axis=1, keepdims=True)[0:1]
+    hot = hot.astype(jnp.float32).astype(jnp.bfloat16)
+    mod_own[...] = jnp.zeros_like(mod_own)
+    mod_own[0:1, :] = dot(hot, mod_table[:, :width])[0:1]
+    mod_own[1:2, :] = 1.0 + dot(hot, mod_table[:, width : 2 * width])[0:1]
+    mod_own[2:3, :] = rate * dot(hot, mod_table[:, 2 * width :])[0:1]
+    gains[0:1, :] = q_gain[...] * (math.log2(math.e) / math.sqrt(HD))
+    gains[1:2, :] = k_gain[...]
+
     arrivals = len(partners)
-    for v in extra.values():
+    for _, v in extra:
         arrivals = arrivals + (q == v).astype(jnp.int32) + (q == last).astype(jnp.int32)
     pl.semaphore_wait(barrier, arrivals)
 
@@ -141,47 +157,69 @@
             )
             noise_copies.append((c, k, copy))
 
-            @pl.when(q == noise_from[k])
+            @pl.when(q == noise_from[k, c])
             def _():
                 copy.start()
 
-    core_half = pl.ds(pl.multiple_of(core * half, HD), half)
-    quarter = half // 2
-    core_quarter = [
-        pl.ds(pl.multiple_of(core * half + j * quarter, HD), quarter) for j in range(2)
-    ]
-
-    def wo_rows(xx):
-        return pl.ds(pl.multiple_of(lax.rem(xx + n_x, n_x) * cols, HD), cols)
-
-    wo_direct = [
-        remote(wout.at[:, core_half], wo.at[own_wo, core_half], dev(tensor=tensor_of(x + d, y)))
-        for d in (1, -1)
-    ]
-    for copy in wo_direct:
+    n_z = n_queue // 4
+    z_side = (q // 4) % 2 if n_z > 1 else 0
+    sides = 2 if n_z > 1 else 1
+    share = width // (2 * sides)
+
+    def share_cols(side, part=None):
+        start = (side * 2 + core) * share
+        if part is None:
+            return pl.ds(pl.multiple_of(start, HD), share)
+        return pl.ds(pl.multiple_of(start + part * (share // 2), HD), share // 2)
+
+    def wo_region(xx, side, part=None, row_part=None):
+        start, size = lax.rem(xx + n_x, n_x) * cols, cols
+        if row_part is not None:
+            start, size = start + row_part * (cols // 2), cols // 2
+        return wo.at[pl.ds(pl.multiple_of(start, 16), size), share_cols(side, part)]
+
+    other_core = q + 1 - 2 * core
+    z_ways = (4, -4)
+    wo_direct, wo_far, wo_pass, wo_z = [], [], [], []
+
+    def wo_move(region, to, into):
+        copy = remote(region, region, to)
         copy.start()
-    other_core = q + 1 - 2 * core
-    wo_far, wo_pass = [], []
+        into.append(copy)
+
+    def wo_start():
+        for d in (1, -1):
+            copy = remote(
+                wout.at[:, share_cols(z_side)], wo.at[own_wo, share_cols(z_side)],
+                dev(tensor=tensor_of(x + d, y)),
+            )
+            copy.start()
+            wo_direct.append(copy)
 
     def wo_forward():
         for i, d in enumerate((1, -1)):
             wo_direct[i].wait_recv()
-            region = wo.at[wo_rows(x - d), core_quarter[i]]
-            copy = remote(region, region, dev(tensor=tensor_of(x + d, y)))
-            copy.start()
-            wo_far.append(copy)
-            region = wo.at[wo_rows(x - d), core_half]
-            copy = remote(region, region, dev(queue=other_core))
-            copy.start()
-            wo_pass.append(copy)
-
-    def wo_finish():
+            wo_move(wo_region(x - d, z_side, part=i), dev(tensor=tensor_of(x + d, y)), wo_far)
+            if sides == 2:
+                for e, dz in enumerate(z_ways):
+                    wo_move(wo_region(x - d, z_side, row_part=e), dev(queue=queue_at(dz)), wo_z)
+            wo_move(wo_region(x - d, z_side), dev(queue=other_core), wo_pass)
+
+    def wo_forward_far():
         for i in range(2):
             wo_far[i].wait_recv()
-            region = wo.at[wo_rows(x + 2), core_quarter[i]]
-            copy = remote(region, region, dev(queue=other_core))
-            copy.start()
-            wo_pass.append(copy)
+            if sides == 2:
+                wo_move(wo_region(x + 2, z_side, part=i), dev(queue=queue_at(z_ways[i])), wo_z)
+        wo_move(wo_region(x + 2, z_side), dev(queue=other_core), wo_pass)
+
+    def wo_other_side():
+        if sides == 2:
+            for i, xx in enumerate((x - 1, x + 1, x + 2)):
+                for e in range(2):
+                    wo_z[2 * i + e].wait_recv()
+                wo_move(wo_region(xx, 1 - z_side), dev(queue=other_core), wo_pass)
+
+    def wo_finish():
         for copy in wo_pass:
             copy.wait_recv()
         load_o.wait()
@@ -382,9 +420,11 @@
                 partials.append(project_out(step, c, k))
         return partials
 
-    def attention(step, position_zero, kv_copies):
+    def attention(step, position_zero, kv_copies, between=()):
         for c in range(chunks):
             attend_own(c)
+            if between and c == 0:
+                between[0]()
         for copy in kv_copies:
             copy.wait_recv()
         exchanged = []
@@ -399,40 +439,42 @@
                 attend_prev(step, c)
 
             exchanged.append(exchange_att(step, c))
+            if between and c == 0:
+                between[1]()
         return exchanged
 
-    @pl.when(q != last)
-    def _():
-        pltpu.make_async_copy(frame0.at[0], frame0.at[0], load_sem.at[0]).wait()
-
-    @pl.when(q == last)
-    def _():
-        for c in range(chunks):
+    def wait_frame(c):
+        @pl.when(q != last)
+        def _():
+            pltpu.make_async_copy(frame0.at[c], frame0.at[c], load_sem.at[c]).wait()
+
+        @pl.when(q == last)
+        def _():
             own_noise[c].wait()
-        for c, k, copy in noise_copies:
-            copy.wait_recv()
-
+            for cc, k, copy in noise_copies:
+                if cc == c:
+                    copy.wait_recv()
+
+    wait_frame(0)
     send_mod.wait_recv()
     norm_chunk(frame0, mod_next, 0)
+    wo_start()
     for copy in load_kv:
         copy.wait()
     kv_copies = []
     project_kv(0)
     kv_copies.append(send_kv(0, 0))
     for c in range(1, chunks):
-
-        @pl.when(q != last)
-        def _():
-            pltpu.make_async_copy(frame0.at[c], frame0.at[c], load_sem.at[c]).wait()
-
+        wait_frame(c)
         norm_chunk(frame0, mod_next, c)
         project_kv(c)
         kv_copies.append(send_kv(0, c))
     load_q.wait()
-    for c in range(chunks):
+    project_q(0)
+    wo_forward()
+    for c in range(1, chunks):
         project_q(c)
-    exchanged = attention(0, q == last, kv_copies)
-    wo_forward()
+    exchanged = attention(0, q == last, kv_copies, (wo_forward_far, wo_other_side))
     wo_finish()
     partials = output_projection(0, exchanged)
 
@@ -524,7 +566,7 @@
         copy.wait_send()
     for c, k, copy in noise_copies:
 
-        @pl.when(q == noise_from[k])
+        @pl.when(q == noise_from[k, c])
         def _():
             copy.wait_send()
 
@@ -539,21 +581,6 @@
     chunks = CHUNKS
     chunk_rows = frame_rows // chunks
     rows = chunk_rows // n_tensor
-    onehot = (jnp.arange(mod_table.shape[0], dtype=jnp.int32) == levels[0]).astype(jnp.bfloat16)
-    modulation = jnp.dot(onehot[None, :], mod_table, preferred_element_type=jnp.float32)
-    rate = jnp.sum(onehot.astype(jnp.float32) * step_size)
-    shift, scale, gate = jnp.split(modulation, 3, axis=1)
-    mod = jnp.concatenate(
-        [shift, 1.0 + scale, rate * gate, jnp.zeros((5, width), jnp.float32)], axis=0
-    )
-    gains = jnp.concatenate(
-        [
-            (q_gain * (math.log2(math.e) / math.sqrt(HD)))[None],
-            k_gain[None],
-            jnp.zeros((6, HD), jnp.float32),
-        ],
-        axis=0,
-    )
     bf16, f32 = jnp.bfloat16, jnp.float32
     frame = pltpu.VMEM((chunks, chunk_rows, width), bf16)
     anywhere = pl.BlockSpec(memory_space=pl.ANY)
@@ -562,7 +589,7 @@
     out = pl.pallas_call(
         kernel,
         out_shape=jax.ShapeDtypeStruct((chunks, chunk_rows, width), bf16),
-        in_specs=[anywhere, anywhere, anywhere, anywhere, vmem, vmem],
+        in_specs=[pl.BlockSpec(memory_space=pltpu.SMEM)] + [anywhere] * 4 + [vmem] * 4,
         out_specs=anywhere,
         scratch_shapes=[
             frame, frame, frame, frame,
@@ -573,6 +600,8 @@
             pltpu.VMEM((2, frame_rows, cols), bf16),
             pltpu.VMEM((STEPS, 2, frame_rows, cols), bf16),
             pltpu.VMEM((8, width), f32),
+            pltpu.VMEM((8, width), f32),
+            pltpu.VMEM((8, HD), f32),
             pltpu.VMEM((chunks, chunk_rows, cols), f32),
             pltpu.VMEM((chunks, heads, chunk_rows, HD), f32),
             pltpu.VMEM((chunks, heads, chunk_rows, HD), f32),
@@ -590,7 +619,10 @@
             collective_id=0, has_side_effects=True, vmem_limit_bytes=62 * 1024 * 1024
         ),
         name="denoise",
-    )(latents, fresh_noise, qkv_weight, out_weight, mod, gains)
+    )(
+        levels, latents, fresh_noise, qkv_weight, out_weight, mod_table,
+        step_size[None], q_gain[None], k_gain[None],
+    )
     out = out.reshape(chunks, n_tensor, rows, width).transpose(1, 0, 2, 3)
     return out.reshape(1, frame_rows, width)
 

time: 204 us -> 193 us (0.946)
  Pallas kernels: 193 us -> 187 us
  other arithmetic: 4.74 us -> 0 us
    pallas_call x1, Pallas kernels: 193 us -> 187 us  [body(): pl.pallas_call(kernel, out_shape=jax.ShapeDtypeStruct((chunks, chunk_rows...]
where the time goes in v3:
time: 193 us
  Pallas kernels  187 us (97%)
  local copies, waits for them, and re-layouts  4.96 us (3%)
    pallas_call x1, Pallas kernels, body(): pl.pallas_call(kernel, out_shape=jax.ShapeDtypeStruct((chunks, chunk_rows...  187 us
    transpose x1, local copies, waits for them, and re-layouts, body(): out = out.reshape(chunks, n_tensor, rows, width).transpose(1, 0, 2, 3)  4.96 us

profile of v3, /device:TPU:16, one launch (start us, length us, event | category | flops | bytes accessed | tf_op | source)
XLA Modules:
  0.0 192.9 jit_solution(6907777387832173938)
XLA Ops:
  0.7 187.3 %denoise.1 = bf16[2,384,3072]{2,1,0:T(8,128)(2,1)} custom-call(s32[1]{0:T(128)S(6)} %copy.11.levels, bf16[1,768,3072]{2,1,0:T(8,128)(2,1)} %lat.1, bf16[2,96,3072]{2,1,0:T(8,128)(2,1)} %noise.1, bf16[3,3072,384]{2,1,0:T(8,128)(2,1)} %wqkv.1, bf16[384,3072]{1,0:T(8,128)(2,1)} %wout.1, bf16[50,9216]{1,0:T(8,128)(2,1)} %mod_table.1, f32[1,50]{1,0:T(1,128)} %bitcast.8, ...), custom_call_target="tpu_custom_call" | custom-call | tf_op jit(solution)/shard_map/denoise/pallas_call | solution.py:589
  188.0 5.0 %copy.10 = bf16[8,2,48,3072]{3,2,1,0:T(8,128)(2,1)} copy(bf16[8,2,48,3072]{3,2,0,1:T(8,128)(2,1)} %bitcast.7) | data formatting | bytes 9437184 | tf_op jit(solution)/shard_map/transpose | solution.py:626

commit v4 on v3

--- a/solution.py
+++ b/solution.py
@@ -12,8 +12,8 @@
 STEPS = 2
 CHUNKS = 2
 PARTS = 2
-LAST_PART = 1536
-LAST_CUT = 1280
+CUT_PART = 1536
+CUT = 1280
 MESH = pl.DeviceIdType.MESH
 NOISE_FROM = {1: (15, 15), 2: (15, 15), 3: (3, 3), 4: (11, 11), 5: (2, 10), 6: (15, 15), 7: (13, 13)}
 
@@ -23,9 +23,9 @@
 
 
 def kernel(
-    levels, lat, noise, wqkv, wout, mod_table, step_size, q_gain, k_gain, out,
-    frame0, frame1, frame2, normed, wkv, wq, wo, q_buf, kv, kv_prev, mod_own, mod_next, gains,
-    acc, top, total, att, att_all, own_part, part_send, part_recv, z_send,
+    levels, lat, noise, wqkv, wout, mod_table, step_size, q_gain, k_gain, frame2,
+    frame0, frame1, normed, wkv, wq, wo, q_buf, kv, kv_prev, mod_own, mod_next, gains,
+    acc, lowest, top, total, att, att_all, own_part, part_send, part_recv, z_send,
     load_sem, send_sem, recv_sem,
 ):
     n_queue, n_tensor = lax.axis_size("queue"), lax.axis_size("tensor")
@@ -135,6 +135,7 @@
     rate = jnp.sum(jnp.where(hot, step_size[...], 0.0), axis=1, keepdims=True)[0:1]
     hot = hot.astype(jnp.float32).astype(jnp.bfloat16)
     mod_own[...] = jnp.zeros_like(mod_own)
+    lowest[...] = jnp.full(lowest.shape, -3e38, jnp.float32)
     mod_own[0:1, :] = dot(hot, mod_table[:, :width])[0:1]
     mod_own[1:2, :] = 1.0 + dot(hot, mod_table[:, width : 2 * width])[0:1]
     mod_own[2:3, :] = rate * dot(hot, mod_table[:, 2 * width :])[0:1]
@@ -225,7 +226,7 @@
         load_o.wait()
 
     def norm_chunk(frame, mod, c):
-        tile = rows
+        tile = chunk_rows // 2
 
         def step(i, _):
             at = pl.ds(pl.multiple_of(i * tile, 16), tile)
@@ -260,50 +261,43 @@
         copy.start()
         return copy
 
-    def scores(c, lanes, keys):
-        return lax.dot_general(
-            q_buf[c, :, lanes], keys, (((1,), (1,)), ((), ())), preferred_element_type=jnp.float32
+    def attend(c, h, keys, values, before):
+        lanes = slice(h * HD, (h + 1) * HD)
+        logits = lax.dot_general(
+            q_buf[c, :, lanes], keys[:, lanes], (((1,), (1,)), ((), ())),
+            preferred_element_type=jnp.float32,
         )
+        peak = jnp.max(logits, axis=-1, keepdims=True)
+        peak = jnp.maximum(before, jnp.broadcast_to(peak, (chunk_rows, HD)))
+        tiled = jnp.concatenate([peak] * (logits.shape[1] // HD), axis=1)
+        raised = jnp.exp2(logits - tiled).astype(jnp.bfloat16)
+        ones = jnp.ones((values.shape[0], HD), jnp.bfloat16)
+        both = dot(raised, jnp.concatenate([values[:, lanes], ones], axis=1))
+        return both[:, :HD], both[:, HD:], peak
 
     def attend_own(c):
-        def one(h, _):
-            lanes = pl.ds(pl.multiple_of(h * HD, HD), HD)
-            logits = scores(c, lanes, kv[0, :, lanes])
-            peak = jnp.max(logits, axis=-1, keepdims=True)
-            raised = jnp.exp2(logits - peak)
-            top[c, h] = jnp.broadcast_to(peak, (chunk_rows, HD))
-            total[c, h] = jnp.broadcast_to(
-                jnp.sum(raised, axis=-1, keepdims=True), (chunk_rows, HD)
+        for h in range(heads):
+            summed, weight, peak = attend(c, h, kv.at[0], kv.at[1], lowest[...])
+            acc[c, :, h * HD : (h + 1) * HD] = summed
+            total[c, h] = weight
+            top[c, h] = peak
+
+    def attend_prev(step, c):
+        for h in range(heads):
+            lanes = slice(h * HD, (h + 1) * HD)
+            before = top[c, h]
+            summed, weight, peak = attend(
+                c, h, kv_prev.at[step, 0], kv_prev.at[step, 1], before
             )
-            acc[c, :, lanes] = dot(raised.astype(jnp.bfloat16), kv[1, :, lanes])
-            return 0
-
-        lax.fori_loop(0, heads, one, 0)
-
-    def attend_prev(step, c):
-        def one(h, _):
-            lanes = pl.ds(pl.multiple_of(h * HD, HD), HD)
-            logits = scores(c, lanes, kv_prev[step, 0, :, lanes])
-            before = top[c, h]
-            peak = jnp.maximum(before[:, 0:1], jnp.max(logits, axis=-1, keepdims=True))
-            raised = jnp.exp2(logits - peak)
             fade = jnp.exp2(before - peak)
-            weight = total[c, h] * fade + jnp.sum(raised, axis=-1, keepdims=True)
-            summed = acc[c, :, lanes] * fade + dot(
-                raised.astype(jnp.bfloat16), kv_prev[step, 1, :, lanes]
-            )
+            weight = total[c, h] * fade + weight
+            summed = acc[c, :, lanes] * fade + summed
             att[step, c, :, lanes] = (summed / weight).astype(jnp.bfloat16)
-            return 0
-
-        lax.fori_loop(0, heads, one, 0)
 
     def attend_alone(step, c):
-        def one(h, _):
-            lanes = pl.ds(pl.multiple_of(h * HD, HD), HD)
+        for h in range(heads):
+            lanes = slice(h * HD, (h + 1) * HD)
             att[step, c, :, lanes] = (acc[c, :, lanes] / total[c, h]).astype(jnp.bfloat16)
-            return 0
-
-        lax.fori_loop(0, heads, one, 0)
 
     def exchange_att(step, c):
         mine = pl.ds(pl.multiple_of(x * cols, HD), cols)
@@ -323,20 +317,14 @@
 
     parts = PARTS
     part_cols = width // parts
-    n_tile = 512 if part_cols % 512 == 0 else HD
     units = [(c, k) for c in range(chunks) for k in range(parts)]
 
     def project_out(step, c, k):
-        def one(i, _):
-            lanes = pl.ds(pl.multiple_of(k * part_cols + i * n_tile, HD), n_tile)
-            part = dot(att_all[step, c], wo[:, lanes])
-            low, high = part[:rows], part[rows:]
-            own_part[c, :, lanes] = jnp.where(y == 0, low, high)
-            part_send[step, c, :, lanes] = jnp.where(y == 0, high, low).astype(jnp.bfloat16)
-            return 0
-
-        lax.fori_loop(0, part_cols // n_tile, one, 0)
         lanes = pl.ds(k * part_cols, part_cols)
+        part = dot(att_all[step, c], wo[:, lanes])
+        low, high = part[:rows], part[rows:]
+        own_part[c, :, lanes] = jnp.where(y == 0, low, high)
+        part_send[step, c, :, lanes] = jnp.where(y == 0, high, low).astype(jnp.bfloat16)
         copy = remote(
             part_send.at[step, c, :, lanes], part_recv.at[step, c, :, lanes], dev(tensor=partner)
         )
@@ -501,6 +489,7 @@
 
     n_units = len(units)
     shifted = [None] * n_units
+    cut = CUT if part_cols == CUT_PART else part_cols // 2
     gathers = [Gather(frame1, c, k, 1 - y, part_cols) for c, k in units]
 
     def first_after_shift(u):
@@ -515,7 +504,7 @@
         if 0 <= tick - 2 < n_units:
             gathers[tick - 2].second()
             gathers[tick - 2].forward_own()
-        if 0 <= tick - 3 < n_units - parts:
+        if 0 <= tick - 3 < parts:
             gathers[tick - 3].forward_other()
 
     for copy in kv_copies:
@@ -523,27 +512,21 @@
     sent[:] = [copy for copy in sent if all(copy is not done for done in kv_copies)]
     kv_copies = []
     for c in range(chunks):
+        if c + 1 < chunks and chunks > 2:
+            for k in range(parts):
+                gathers[(c + 1) * parts + k].forward_other()
         for k in range(parts):
             gathers[c * parts + k].wait()
         norm_chunk(frame1, mod_own, c)
         project_kv(c)
         kv_copies.append(send_kv(1, c))
-        if c == chunks - 2:
-            for u in range(n_units - parts, n_units):
-                gathers[u].forward_other()
+        if c + 1 < chunks and chunks == 2:
+            for k in range(parts):
+                gathers[(c + 1) * parts + k].forward_other()
         project_q(c)
     exchanged = attention(1, q == 0, kv_copies)
     partials = output_projection(1, exchanged)
-    cut = LAST_CUT if part_cols == LAST_PART else part_cols // 2
     gathers = [Gather(frame2, c, k, y, cut) for c, k in units]
-    stores = []
-
-    def store(c):
-        for k in range(parts):
-            gathers[c * parts + k].wait()
-        copy = load(frame2.at[c], out.at[c], c)
-        copy.start()
-        stores.append(copy)
 
     for tick in range(n_units + 2):
         if tick < n_units:
@@ -558,10 +541,8 @@
             gathers[tick - 1].forward_own()
         if 0 <= tick - 2 < n_units:
             gathers[tick - 2].forward_other()
-    for c in range(chunks):
-        store(c)
-    for copy in stores:
-        copy.wait()
+    for gather in gathers:
+        gather.wait()
     for copy in sent:
         copy.wait_send()
     for c, k, copy in noise_copies:
@@ -585,14 +566,14 @@
     frame = pltpu.VMEM((chunks, chunk_rows, width), bf16)
     anywhere = pl.BlockSpec(memory_space=pl.ANY)
     vmem = pl.BlockSpec(memory_space=pltpu.VMEM)
-    n_copies = 192
+    n_copies = 256
     out = pl.pallas_call(
         kernel,
-        out_shape=jax.ShapeDtypeStruct((chunks, chunk_rows, width), bf16),
+        out_shape=pltpu.VMEM((chunks, chunk_rows, width), bf16),
         in_specs=[pl.BlockSpec(memory_space=pltpu.SMEM)] + [anywhere] * 4 + [vmem] * 4,
-        out_specs=anywhere,
+        out_specs=vmem,
         scratch_shapes=[
-            frame, frame, frame, frame,
+            frame, frame, frame,
             pltpu.VMEM((width, 2 * cols), bf16),
             pltpu.VMEM((width, cols), bf16),
             pltpu.VMEM((n_tensor // 2 * cols, width), bf16),
@@ -603,6 +584,7 @@
             pltpu.VMEM((8, width), f32),
             pltpu.VMEM((8, HD), f32),
             pltpu.VMEM((chunks, chunk_rows, cols), f32),
+            pltpu.VMEM((chunk_rows, HD), f32),
             pltpu.VMEM((chunks, heads, chunk_rows, HD), f32),
             pltpu.VMEM((chunks, heads, chunk_rows, HD), f32),
             pltpu.VMEM((STEPS, chunks, chunk_rows, cols), bf16),
@@ -616,7 +598,7 @@
             pltpu.SemaphoreType.DMA((n_copies,)),
         ],
         compiler_params=pltpu.CompilerParams(
-            collective_id=0, has_side_effects=True, vmem_limit_bytes=62 * 1024 * 1024
+            collective_id=0, has_side_effects=True, vmem_limit_bytes=54 * 1024 * 1024
         ),
         name="denoise",
     )(

time: 193 us -> 185 us (0.959)
  Pallas kernels: 187 us -> 181 us
  local copies, waits for them, and re-layouts: 4.96 us -> 2.63 us
    pallas_call x1, Pallas kernels: 187 us -> 181 us  [body(): pl.pallas_call(kernel, out_shape=pltpu.VMEM((chunks, chunk_rows, width),...]
    transpose x1, local copies, waits for them, and re-layouts: 4.96 us -> 2.63 us  [body(): out = out.reshape(chunks, n_tensor, rows, width).transpose(1, 0, 2, 3)]
where the time goes in v4:
time: 185 us
  Pallas kernels  181 us (98%)
  local copies, waits for them, and re-layouts  2.63 us (1%)
    pallas_call x1, Pallas kernels, body(): pl.pallas_call(kernel, out_shape=pltpu.VMEM((chunks, chunk_rows, width),...  181 us

profile of v4, /device:TPU:16, one launch (start us, length us, event | category | flops | bytes accessed | tf_op | source)
XLA Modules:
  0.0 184.6 jit_solution(670352618718342038)
XLA Ops:
  0.7 181.3 %denoise.1 = bf16[2,384,3072]{2,1,0:T(8,128)(2,1)S(1)} custom-call(s32[1]{0:T(128)S(6)} %copy.11.levels, bf16[1,768,3072]{2,1,0:T(8,128)(2,1)} %lat.1, bf16[2,96,3072]{2,1,0:T(8,128)(2,1)} %noise.1, bf16[3,3072,384]{2,1,0:T(8,128)(2,1)} %wqkv.1, bf16[384,3072]{1,0:T(8,128)(2,1)} %wout.1, bf16[50,9216]{1,0:T(8,128)(2,1)} %mod_table.1, f32[1,50]{1,0:T(1,128)} %bitcast.8, ...), custom_call_target="tpu_custom_call" | custom-call | tf_op jit(solution)/shard_map/denoise/pallas_call | solution.py:570
  182.0 2.6 %copy.10 = bf16[8,2,48,3072]{3,2,1,0:T(8,128)(2,1)} copy(bf16[8,2,48,3072]{3,2,0,1:T(8,128)(2,1)S(1)} %bitcast.7) | data formatting | bytes 9437184 | tf_op jit(solution)/shard_map/transpose | solution.py:608

commit v5 on v4

--- a/solution.py
+++ b/solution.py
@@ -189,35 +189,40 @@
         into.append(copy)
 
     def wo_start():
-        for d in (1, -1):
-            copy = remote(
-                wout.at[:, share_cols(z_side)], wo.at[own_wo, share_cols(z_side)],
-                dev(tensor=tensor_of(x + d, y)),
+        for e in range(2):
+            row_half = pl.ds(e * (cols // 2), cols // 2)
+            for d in (1, -1):
+                copy = remote(
+                    wout.at[row_half, share_cols(z_side)], wo_region(x, z_side, row_part=e),
+                    dev(tensor=tensor_of(x + d, y)),
+                )
+                copy.start()
+                wo_direct.append(copy)
+
+    def wo_forward(e):
+        for i, d in enumerate((1, -1)):
+            wo_direct[2 * e + i].wait_recv()
+            wo_move(
+                wo_region(x - d, z_side, part=i, row_part=e), dev(tensor=tensor_of(x + d, y)), wo_far
             )
-            copy.start()
-            wo_direct.append(copy)
-
-    def wo_forward():
-        for i, d in enumerate((1, -1)):
-            wo_direct[i].wait_recv()
-            wo_move(wo_region(x - d, z_side, part=i), dev(tensor=tensor_of(x + d, y)), wo_far)
+            region = wo_region(x - d, z_side, row_part=e)
             if sides == 2:
-                for e, dz in enumerate(z_ways):
-                    wo_move(wo_region(x - d, z_side, row_part=e), dev(queue=queue_at(dz)), wo_z)
-            wo_move(wo_region(x - d, z_side), dev(queue=other_core), wo_pass)
+                wo_move(region, dev(queue=queue_at(z_ways[(i + e) % 2])), wo_z)
+            wo_move(region, dev(queue=other_core), wo_pass)
 
     def wo_forward_far():
         for i in range(2):
-            wo_far[i].wait_recv()
+            for e in range(2):
+                wo_far[2 * e + i].wait_recv()
             if sides == 2:
                 wo_move(wo_region(x + 2, z_side, part=i), dev(queue=queue_at(z_ways[i])), wo_z)
         wo_move(wo_region(x + 2, z_side), dev(queue=other_core), wo_pass)
 
     def wo_other_side():
+        for copy in wo_z:
+            copy.wait_recv()
         if sides == 2:
-            for i, xx in enumerate((x - 1, x + 1, x + 2)):
-                for e in range(2):
-                    wo_z[2 * i + e].wait_recv()
+            for xx in (x - 1, x + 1, x + 2):
                 wo_move(wo_region(xx, 1 - z_side), dev(queue=other_core), wo_pass)
 
     def wo_finish():
@@ -408,11 +413,11 @@
                 partials.append(project_out(step, c, k))
         return partials
 
-    def attention(step, position_zero, kv_copies, between=()):
+    def attention(step, position_zero, kv_copies, between=None):
         for c in range(chunks):
             attend_own(c)
-            if between and c == 0:
-                between[0]()
+            if between is not None and c == 0:
+                between()
         for copy in kv_copies:
             copy.wait_recv()
         exchanged = []
@@ -427,8 +432,6 @@
                 attend_prev(step, c)
 
             exchanged.append(exchange_att(step, c))
-            if between and c == 0:
-                between[1]()
         return exchanged
 
     def wait_frame(c):
@@ -443,10 +446,10 @@
                 if cc == c:
                     copy.wait_recv()
 
+    wo_start()
     wait_frame(0)
     send_mod.wait_recv()
     norm_chunk(frame0, mod_next, 0)
-    wo_start()
     for copy in load_kv:
         copy.wait()
     kv_copies = []
@@ -457,12 +460,14 @@
         norm_chunk(frame0, mod_next, c)
         project_kv(c)
         kv_copies.append(send_kv(0, c))
+    wo_forward(0)
     load_q.wait()
     project_q(0)
-    wo_forward()
+    wo_forward(1)
     for c in range(1, chunks):
         project_q(c)
-    exchanged = attention(0, q == last, kv_copies, (wo_forward_far, wo_other_side))
+    exchanged = attention(0, q == last, kv_copies, wo_forward_far)
+    wo_other_side()
     wo_finish()
     partials = output_projection(0, exchanged)
 

time: 185 us -> 179 us (0.968); the launches traced: 185 us -> 176 us
  Pallas kernels: 181 us -> 173 us
    pallas_call x1, Pallas kernels: 181 us -> 173 us  [body(): pl.pallas_call(kernel, out_shape=pltpu.VMEM((chunks, chunk_rows, width),...]
where the time goes in v5:
time: 179 us; the launch traced here: 176 us
  Pallas kernels  173 us (97%)
  local copies, waits for them, and re-layouts  2.63 us (1%)
    pallas_call x1, Pallas kernels, body(): pl.pallas_call(kernel, out_shape=pltpu.VMEM((chunks, chunk_rows, width),...  173 us

profile of v5, /device:TPU:16, one launch (start us, length us, event | category | flops | bytes accessed | tf_op | source)
XLA Modules:
  0.0 176.0 jit_solution(16858117683491195993)
XLA Ops:
  0.7 172.7 %denoise.1 = bf16[2,384,3072]{2,1,0:T(8,128)(2,1)S(1)} custom-call(s32[1]{0:T(128)S(6)} %copy.11.levels, bf16[1,768,3072]{2,1,0:T(8,128)(2,1)} %lat.1, bf16[2,96,3072]{2,1,0:T(8,128)(2,1)} %noise.1, bf16[3,3072,384]{2,1,0:T(8,128)(2,1)} %wqkv.1, bf16[384,3072]{1,0:T(8,128)(2,1)} %wout.1, bf16[50,9216]{1,0:T(8,128)(2,1)} %mod_table.1, f32[1,50]{1,0:T(1,128)} %bitcast.8, ...), custom_call_target="tpu_custom_call" | custom-call | tf_op jit(solution)/shard_map/denoise/pallas_call | solution.py:575
  173.3 2.6 %copy.10 = bf16[8,2,48,3072]{3,2,1,0:T(8,128)(2,1)} copy(bf16[8,2,48,3072]{3,2,0,1:T(8,128)(2,1)S(1)} %bitcast.7) | data formatting | bytes 9437184 | tf_op jit(solution)/shard_map/transpose | solution.py:613
